TPU v7x, 32 devices: a whole 2x2x4 slice. The times are simulated.
32 devices in a mesh: fsdp: 32 (over z, y, x, core).
Axes of the slice: x: 2, y: 2, z: 4, core: 2. Of those that a mesh axis runs over, the one named last changes fastest.
Arguments:
- tokens: bfloat16 [65536, 768], P('fsdp'), may hold values from -6 to 6
- seq_lengths: int32 [32, 2, 4], P('fsdp'), may hold values from 0 to 1024, as said below
- query_weight: bfloat16 [768, 768], P('fsdp'), may hold values from -0.21875 to 0.21875
- query_bias: bfloat16 [768], P('fsdp'), may hold values from -3 to 3
- key_weight: bfloat16 [768, 768], P('fsdp'), may hold values from -0.21875 to 0.21875
- value_weight: bfloat16 [768, 768], P('fsdp'), may hold values from -0.21875 to 0.21875
- value_bias: bfloat16 [768], P('fsdp'), may hold values from -3 to 3
- output_weight: bfloat16 [768, 768], P('fsdp'), may hold values from -0.875 to 0.875
- output_bias: bfloat16 [768], P('fsdp'), may hold values from -3 to 3
- first_gain: bfloat16 [768], P('fsdp'), may hold values from 0.099609375 to 1.8984375
- first_shift: bfloat16 [768], P('fsdp'), may hold values from -3 to 3
- up_weight: bfloat16 [768, 3072], P('fsdp'), may hold values from -0.21875 to 0.21875
- up_bias: bfloat16 [3072], P('fsdp'), may hold values from -3 to 3
- down_weight: bfloat16 [3072, 768], P('fsdp'), may hold values from -0.109375 to 0.109375
- down_bias: bfloat16 [768], P('fsdp'), may hold values from -3 to 3
- second_gain: bfloat16 [768], P('fsdp'), may hold values from 0.099609375 to 1.8984375
- second_shift: bfloat16 [768], P('fsdp'), may hold values from -3 to 3
- cotangent: bfloat16 [65536, 768], P('fsdp'), may hold values from -6 to 6
Outputs:
- layer_output: bfloat16 [65536, 768], P('fsdp')
- token_gradient: float32 [65536, 768], P('fsdp')
- query_weight_gradient: float32 [768, 768], P('fsdp')
- query_bias_gradient: float32 [768], P('fsdp')
- key_weight_gradient: float32 [768, 768], P('fsdp')
- value_weight_gradient: float32 [768, 768], P('fsdp')
- value_bias_gradient: float32 [768], P('fsdp')
- output_weight_gradient: float32 [768, 768], P('fsdp')
- output_bias_gradient: float32 [768], P('fsdp')
- first_gain_gradient: float32 [768], P('fsdp')
- first_shift_gradient: float32 [768], P('fsdp')
- up_weight_gradient: float32 [768, 3072], P('fsdp')
- up_bias_gradient: float32 [3072], P('fsdp')
- down_weight_gradient: float32 [3072, 768], P('fsdp')
- down_bias_gradient: float32 [768], P('fsdp')
- second_gain_gradient: float32 [768], P('fsdp')
- second_shift_gradient: float32 [768], P('fsdp')
Inputs may be any that keep to these rules, and one draw needn't show every extreme that they name: Each row seq_lengths[d, m, :] lists, in order, the sequences packed into slot m of device d: either one sequence of exactly 1024 tokens followed by zeros, or 4 sequences of 128 to 256 tokens each, or all zeros for an unused slot. A device's used slots come first and it uses 1 to 2 of them; some slot holds a sequence of exactly 1024 tokens and some device uses all 2 slots.
All inputs are finite; a program needn't handle non-finite values.
Results may differ from a plain program's by a relative error of at most 0.014.
Values may be sent and summed in bfloat16 or wider, within the bound.
A program may use at most 192 MiB of HBM per device.

v0:
```python
import math

import jax
import jax.numpy as jnp
from jax import lax
from jax.sharding import PartitionSpec as P

H = 12
HD = 64


epsilon = 1e-05
neg_fill = -1e30


def segments(lengths, length):
    bounds = jnp.cumsum(lengths, dtype=jnp.int32)
    places = jnp.arange(length, dtype=jnp.int32)
    labels = jnp.sum((places[:, None] >= bounds[None, :]).astype(jnp.int32), axis=1)
    live = (places < bounds[-1]).astype(jnp.float32)
    return (labels[:, None] == labels[None, :], live)


def normalize(rows):
    center = rows - jnp.mean(rows, axis=-1, keepdims=True)
    scale = lax.rsqrt(jnp.mean(center * center, axis=-1, keepdims=True) + epsilon)
    return (center * scale, scale)


def norm_back(incoming, normed, scale):
    return scale * (
        incoming
        - jnp.mean(incoming, axis=-1, keepdims=True)
        - normed * jnp.mean(incoming * normed, axis=-1, keepdims=True)
    )


def gelu_slope(upward):
    return 0.5 * (1.0 + lax.erf(upward * (1.0 / math.sqrt(2.0)))) + upward * jnp.exp(
        -0.5 * upward * upward
    ) * (1.0 / math.sqrt(2.0 * math.pi))


def merge_heads(stacked, length):
    return jnp.transpose(stacked, (1, 0, 2, 3)).reshape(length, -1)


def rows_outer(left, right):
    return jnp.einsum("ti,tj->ij", left, right, preferred_element_type=jnp.float32)


def times_transposed(left, right):
    return jnp.einsum("tj,ij->ti", left, right, preferred_element_type=jnp.float32)


def pair_scores(query, keys, same, index):
    query_pair = lax.dynamic_slice_in_dim(query, 2 * index, 2, 1)
    keys_pair = lax.dynamic_slice_in_dim(keys, 2 * index, 2, 1)
    scores = jnp.einsum("qhd,khd->hqk", query_pair, keys_pair, preferred_element_type=jnp.float32)
    scores = scores * query.shape[2] ** (-0.5)
    return (jnp.where(same[None], scores, neg_fill), query_pair, keys_pair)


def attend_forward(query, keys, values, same):

    def one_pair(index):
        scores, query_pair, keys_pair = pair_scores(query, keys, same, index)
        values_pair = lax.dynamic_slice_in_dim(values, 2 * index, 2, 1)
        top = jnp.max(scores, axis=-1, keepdims=True)
        raised = jnp.exp(scores - top)
        total = jnp.sum(raised, axis=-1, keepdims=True)
        shares = (raised / total).astype(jnp.bfloat16)
        mixed = jnp.einsum("hqk,khd->qhd", shares, values_pair, preferred_element_type=jnp.float32)
        return (mixed, (top + jnp.log(total))[..., 0])

    return lax.map(one_pair, jnp.arange(query.shape[1] // 2, dtype=jnp.int32))


def attend_backward(query, keys, values, upstream, same, log_total):
    scale = query.shape[2] ** (-0.5)

    def one_pair(index):
        scores, query_pair, keys_pair = pair_scores(query, keys, same, index)
        values_pair = lax.dynamic_slice_in_dim(values, 2 * index, 2, 1)
        upstream_pair = lax.dynamic_slice_in_dim(upstream, 2 * index, 2, 1)
        shares = jnp.exp(scores - log_total[index][:, :, None])
        product = jnp.einsum(
            "qhd,khd->hqk", upstream_pair, values_pair, preferred_element_type=jnp.float32
        )
        inner = jnp.sum(shares * product, axis=-1, keepdims=True)
        score_back = (shares * (product - inner)).astype(jnp.bfloat16)
        query_back = (
            jnp.einsum("hqk,khd->qhd", score_back, keys_pair, preferred_element_type=jnp.float32)
            * scale
        )
        keys_back = (
            jnp.einsum("hqk,qhd->khd", score_back, query_pair, preferred_element_type=jnp.float32)
            * scale
        )
        values_back = jnp.einsum(
            "hqk,qhd->khd",
            shares.astype(jnp.bfloat16),
            upstream_pair,
            preferred_element_type=jnp.float32,
        )
        return (query_back, keys_back, values_back)

    return lax.map(one_pair, jnp.arange(query.shape[1] // 2, dtype=jnp.int32))


def layer_forward(rows, lengths, weights):
    (
        query_weight,
        query_bias,
        key_weight,
        value_weight,
        value_bias,
        output_weight,
        output_bias,
        first_gain,
        first_shift,
        up_weight,
        up_bias,
        down_weight,
        down_bias,
        second_gain,
        second_shift,
    ) = weights
    length = rows.shape[0]
    same, live = segments(lengths, length)
    query = (jnp.dot(rows, query_weight, preferred_element_type=jnp.float32) + query_bias).astype(
        jnp.bfloat16
    )
    keys = jnp.dot(rows, key_weight, preferred_element_type=jnp.float32).astype(jnp.bfloat16)
    values = (jnp.dot(rows, value_weight, preferred_element_type=jnp.float32) + value_bias).astype(
        jnp.bfloat16
    )
    query = query.reshape(length, H, HD)
    keys = keys.reshape(length, H, HD)
    values = values.reshape(length, H, HD)
    mixed, log_total = attend_forward(query, keys, values, same)
    attended = merge_heads(mixed, length).astype(jnp.bfloat16)
    first = (
        rows.astype(jnp.float32)
        + jnp.dot(attended, output_weight, preferred_element_type=jnp.float32)
        + output_bias
    )
    normed_one, scale_one = normalize(first)
    hidden = normed_one * first_gain + first_shift
    hidden_low = hidden.astype(jnp.bfloat16)
    upward = jnp.dot(hidden_low, up_weight, preferred_element_type=jnp.float32) + up_bias
    active = jax.nn.gelu(upward, approximate=False).astype(jnp.bfloat16)
    second = hidden + jnp.dot(active, down_weight, preferred_element_type=jnp.float32) + down_bias
    normed_two, scale_two = normalize(second)
    result = ((normed_two * second_gain + second_shift) * live[:, None]).astype(jnp.bfloat16)
    kept = (
        same,
        live,
        query,
        keys,
        values,
        log_total,
        attended,
        normed_one,
        scale_one,
        hidden_low,
        upward,
        active,
        normed_two,
        scale_two,
    )
    return (kept, result)


def layer_backward(rows, upstream_rows, kept, weights):
    (
        query_weight,
        query_bias,
        key_weight,
        value_weight,
        value_bias,
        output_weight,
        output_bias,
        first_gain,
        first_shift,
        up_weight,
        up_bias,
        down_weight,
        down_bias,
        second_gain,
        second_shift,
    ) = weights
    (
        same,
        live,
        query,
        keys,
        values,
        log_total,
        attended,
        normed_one,
        scale_one,
        hidden_low,
        upward,
        active,
        normed_two,
        scale_two,
    ) = kept
    length = rows.shape[0]
    upstream = upstream_rows.astype(jnp.float32) * live[:, None]
    second_shift_back = jnp.sum(upstream, axis=0)
    second_gain_back = jnp.sum(upstream * normed_two, axis=0)
    second_back = norm_back(upstream * second_gain, normed_two, scale_two)
    mix_low = second_back.astype(jnp.bfloat16)
    down_weight_back = rows_outer(active, mix_low)
    down_bias_back = jnp.sum(mix_low.astype(jnp.float32), axis=0)
    up_low = (times_transposed(mix_low, down_weight) * gelu_slope(upward)).astype(jnp.bfloat16)
    up_weight_back = rows_outer(hidden_low, up_low)
    up_bias_back = jnp.sum(up_low.astype(jnp.float32), axis=0)
    hidden_back = second_back + times_transposed(up_low, up_weight)
    first_shift_back = jnp.sum(hidden_back, axis=0)
    first_gain_back = jnp.sum(hidden_back * normed_one, axis=0)
    first_back = norm_back(hidden_back * first_gain, normed_one, scale_one)
    out_low = first_back.astype(jnp.bfloat16)
    output_weight_back = rows_outer(attended, out_low)
    output_bias_back = jnp.sum(out_low.astype(jnp.float32), axis=0)
    attended_back = (
        times_transposed(out_low, output_weight).astype(jnp.bfloat16).reshape(length, H, HD)
    )
    query_parts, key_parts, value_parts = attend_backward(
        query, keys, values, attended_back, same, log_total
    )
    query_low = merge_heads(query_parts, length).astype(jnp.bfloat16)
    key_low = merge_heads(key_parts, length).astype(jnp.bfloat16)
    value_low = merge_heads(value_parts, length).astype(jnp.bfloat16)
    query_weight_back = rows_outer(rows, query_low)
    query_bias_back = jnp.sum(query_low.astype(jnp.float32), axis=0)
    key_weight_back = rows_outer(rows, key_low)
    value_weight_back = rows_outer(rows, value_low)
    value_bias_back = jnp.sum(value_low.astype(jnp.float32), axis=0)
    rows_back = (
        first_back
        + times_transposed(query_low, query_weight)
        + times_transposed(key_low, key_weight)
        + times_transposed(value_low, value_weight)
    )
    gradients = (
        query_weight_back,
        query_bias_back,
        key_weight_back,
        value_weight_back,
        value_bias_back,
        output_weight_back,
        output_bias_back,
        first_gain_back,
        first_shift_back,
        up_weight_back,
        up_bias_back,
        down_weight_back,
        down_bias_back,
        second_gain_back,
        second_shift_back,
    )
    return (rows_back, gradients)


def on_device(
    tokens,
    seq_lengths,
    query_weight,
    query_bias,
    key_weight,
    value_weight,
    value_bias,
    output_weight,
    output_bias,
    first_gain,
    first_shift,
    up_weight,
    up_bias,
    down_weight,
    down_bias,
    second_gain,
    second_shift,
    cotangent,
):
    shards = (
        query_weight,
        query_bias,
        key_weight,
        value_weight,
        value_bias,
        output_weight,
        output_bias,
        first_gain,
        first_shift,
        up_weight,
        up_bias,
        down_weight,
        down_bias,
        second_gain,
        second_shift,
    )
    width = lax.axis_size("fsdp")
    slots = seq_lengths.shape[1]
    length = tokens.shape[0] // slots
    totals = [
        jnp.zeros((piece.shape[0] * width,) + piece.shape[1:], jnp.float32) for piece in shards
    ]
    outputs = []
    backs = []
    for slot in range(slots):
        rows = lax.slice_in_dim(tokens, slot * length, (slot + 1) * length, axis=0)
        upstream_rows = lax.slice_in_dim(cotangent, slot * length, (slot + 1) * length, axis=0)
        lengths = seq_lengths[0, slot]
        forward_weights = (
            lax.all_gather(query_weight, "fsdp", axis=0, tiled=True),
            lax.all_gather(query_bias, "fsdp", axis=0, tiled=True),
            lax.all_gather(key_weight, "fsdp", axis=0, tiled=True),
            lax.all_gather(value_weight, "fsdp", axis=0, tiled=True),
            lax.all_gather(value_bias, "fsdp", axis=0, tiled=True),
            lax.all_gather(output_weight, "fsdp", axis=0, tiled=True),
            lax.all_gather(output_bias, "fsdp", axis=0, tiled=True),
            lax.all_gather(first_gain, "fsdp", axis=0, tiled=True),
            lax.all_gather(first_shift, "fsdp", axis=0, tiled=True),
            lax.all_gather(up_weight, "fsdp", axis=0, tiled=True),
            lax.all_gather(up_bias, "fsdp", axis=0, tiled=True),
            lax.all_gather(down_weight, "fsdp", axis=0, tiled=True),
            lax.all_gather(down_bias, "fsdp", axis=0, tiled=True),
            lax.all_gather(second_gain, "fsdp", axis=0, tiled=True),
            lax.all_gather(second_shift, "fsdp", axis=0, tiled=True),
        )
        kept, result = layer_forward(rows, lengths, forward_weights)
        outputs.append(result)
        backward_weights = (
            lax.all_gather(query_weight, "fsdp", axis=0, tiled=True),
            lax.all_gather(query_bias, "fsdp", axis=0, tiled=True),
            lax.all_gather(key_weight, "fsdp", axis=0, tiled=True),
            lax.all_gather(value_weight, "fsdp", axis=0, tiled=True),
            lax.all_gather(value_bias, "fsdp", axis=0, tiled=True),
            lax.all_gather(output_weight, "fsdp", axis=0, tiled=True),
            lax.all_gather(output_bias, "fsdp", axis=0, tiled=True),
            lax.all_gather(first_gain, "fsdp", axis=0, tiled=True),
            lax.all_gather(first_shift, "fsdp", axis=0, tiled=True),
            lax.all_gather(up_weight, "fsdp", axis=0, tiled=True),
            lax.all_gather(up_bias, "fsdp", axis=0, tiled=True),
            lax.all_gather(down_weight, "fsdp", axis=0, tiled=True),
            lax.all_gather(down_bias, "fsdp", axis=0, tiled=True),
            lax.all_gather(second_gain, "fsdp", axis=0, tiled=True),
            lax.all_gather(second_shift, "fsdp", axis=0, tiled=True),
        )
        rows_back, gradients = layer_backward(rows, upstream_rows, kept, backward_weights)
        backs.append(rows_back)
        totals = [older + newer for older, newer in zip(totals, gradients)]
    totals = (
        lax.psum_scatter(totals[0], "fsdp", scatter_dimension=0, tiled=True),
        lax.psum_scatter(totals[1], "fsdp", scatter_dimension=0, tiled=True),
        lax.psum_scatter(totals[2], "fsdp", scatter_dimension=0, tiled=True),
        lax.psum_scatter(totals[3], "fsdp", scatter_dimension=0, tiled=True),
        lax.psum_scatter(totals[4], "fsdp", scatter_dimension=0, tiled=True),
        lax.psum_scatter(totals[5], "fsdp", scatter_dimension=0, tiled=True),
        lax.psum_scatter(totals[6], "fsdp", scatter_dimension=0, tiled=True),
        lax.psum_scatter(totals[7], "fsdp", scatter_dimension=0, tiled=True),
        lax.psum_scatter(totals[8], "fsdp", scatter_dimension=0, tiled=True),
        lax.psum_scatter(totals[9], "fsdp", scatter_dimension=0, tiled=True),
        lax.psum_scatter(totals[10], "fsdp", scatter_dimension=0, tiled=True),
        lax.psum_scatter(totals[11], "fsdp", scatter_dimension=0, tiled=True),
        lax.psum_scatter(totals[12], "fsdp", scatter_dimension=0, tiled=True),
        lax.psum_scatter(totals[13], "fsdp", scatter_dimension=0, tiled=True),
        lax.psum_scatter(totals[14], "fsdp", scatter_dimension=0, tiled=True),
    )
    layer_output = jnp.concatenate(outputs, axis=0)
    token_gradient = jnp.concatenate(backs, axis=0)
    return (layer_output, token_gradient) + tuple(totals)


def solution(mesh):
    return jax.shard_map(
        on_device,
        mesh=mesh,
        in_specs=(
            P("fsdp", None),
            P("fsdp", None, None),
            P("fsdp", None),
            P("fsdp"),
            P("fsdp", None),
            P("fsdp", None),
            P("fsdp"),
            P("fsdp", None),
            P("fsdp"),
            P("fsdp"),
            P("fsdp"),
            P("fsdp", None),
            P("fsdp"),
            P("fsdp", None),
            P("fsdp"),
            P("fsdp"),
            P("fsdp"),
            P("fsdp", None),
        ),
        out_specs=(
            P("fsdp", None),
            P("fsdp", None),
            P("fsdp", None),
            P("fsdp"),
            P("fsdp", None),
            P("fsdp", None),
            P("fsdp"),
            P("fsdp", None),
            P("fsdp"),
            P("fsdp"),
            P("fsdp"),
            P("fsdp", None),
            P("fsdp"),
            P("fsdp", None),
            P("fsdp"),
            P("fsdp"),
            P("fsdp"),
        ),
        check_vma=False,
    )
```

profile of v0, /device:TPU:0, one launch (start us, length us, event | category | flops | bytes accessed | tf_op | source)
XLA Modules:
  0.0 1482.4 jit_solution(3848727074629983650)
XLA Ops:
  18.8 42.4 %all-reduce.19 = (bf16[768]{0:T(1024)(128)(2,1)S(1)}, bf16[768]{0:T(1024)(128)(2,1)S(1)}, bf16[768]{0:T(1024)(128)(2,1)S(1)}, bf16[768]{0:T(1024)(128)(2,1)S(1)}...) all-reduce(bf16[768]{0:T(1024)(128)(2,1)S(1)} %dynamic-update-slice, ...), channel_id=1, replica_groups=mesh['fsdp'=32] {'fsdp'}, use_global_device_ids=true, to_apply=%add | all-reduce | flops 9216 | bytes 36864
  72.9 51.0 %all-gather.7.cloned.1.call-done = bf16[768,768]{1,0:T(8,128)(2,1)} async-done(((bf16[24,768]{1,0:T(8,128)(2,1)}), bf16[768,768]{1,0:T(8,128)(2,1)}) %all-gather.7.cloned.1.call-update) | async-done | bytes 1179664 | tf_op jit(solution)/shard_map/all_gather | solution.py:320
  128.3 51.6 %all-gather.9.cloned.1.call-done = bf16[768,768]{1,0:T(8,128)(2,1)} async-done(((bf16[24,768]{1,0:T(8,128)(2,1)}), bf16[768,768]{1,0:T(8,128)(2,1)}) %all-gather.9.cloned.1.call-update) | async-done | bytes 1179664 | tf_op jit(solution)/shard_map/all_gather | solution.py:317
  184.4 63.6 %while.57 = (s32[]{:T(128)}, bf16[6,1024,2,64]{1,3,2,0:T(8,128)(2,1)S(1)}, f32[6,2,1024]{2,1,0:T(2,128)S(1)}, s32[6]{0:T(128)S(1)}, bf16[1024,12,64]{0,2,1:T(8,1...) while((s32[]{:T(128)}, ...), condition=%wide.region_15.16_spmd.clone, body=%wide.region_12.15_spmd.clone.sunk | while | flops 563083264 | bytes 30742200 | solution.py:76
  265.1 77.6 %while.56 = (s32[]{:T(128)}, bf16[6,1024,2,64]{1,3,2,0:T(8,128)(2,1)}, f32[6,2,1024]{2,1,0:T(2,128)S(1)}, s32[6]{0:T(128)S(1)}, bf16[1024,12,64]{0,2,1:T(8,128)(...) while((s32[]{:T(128)}, ...), condition=%wide.region_5.6_spmd.clone, body=%wide.region_2.5_spmd.clone.sunk | while | flops 563083264 | bytes 30742200 | solution.py:76
  348.9 7.4 fusion.162
  360.9 61.6 %fusion.96 = (bf16[1024,3072]{1,0:T(8,128)(2,1)}, bf16[1024,3072]{1,0:T(8,128)(2,1)}, f32[1024,3072]{1,0:T(8,128)}) fusion(f32[3072]{0:T(1024)S(1)} %copy-done.65, f32[1024,3072]{1,0:T(8,128)S(1)} %fusion.162, bf16[768,3072]{1,0:T(8,128)(2,1)S(1)} %copy-done.74, f32[1024,768]{1,0:T(8,128)S(1)} %copy-done.6, f32[768]{0:T(1024)S(1)} %copy-done.40, ...), kind=kOutput, calls=%fused_computation.110 | convolution fusion | flops 5251006464 | bytes 45639680 | tf_op jit(solution)/shard_map/dot_general | solution.py:151
  422.6 9.7 fusion.171
  434.2 5.4 fusion.170
  450.4 14.1 convert_reduce_fusion.1
  464.6 12.6 multiply_reduce_fusion.5
  477.2 12.5 convert_reduce_fusion
  489.7 14.6 convert_reduce_fusion.5
  521.8 179.5 %while.58 = (s32[]{:T(128)}, bf16[6,1024,2,64]{1,3,2,0:T(8,128)(2,1)}, bf16[6,1024,2,64]{1,3,2,0:T(8,128)(2,1)}, bf16[6,1024,2,64]{1,3,2,0:T(8,128)(2,1)}, s32[6...) while((s32[]{:T(128)}, ...), condition=%wide.region_26.27_spmd.clone, body=%wide.region_24.26_spmd.clone.sunk | while | flops 1374943232 | bytes 108330856 | solution.py:108
  523.0 5.6 fusion.277
  531.9 6.8 multiply_reduce_fusion.18
  553.1 5.6 fusion.277
  562.0 6.7 multiply_reduce_fusion.18
  583.0 5.6 fusion.277
  591.9 6.7 multiply_reduce_fusion.18
  612.9 5.6 fusion.277
  621.8 6.7 multiply_reduce_fusion.18
  642.8 5.6 fusion.277
  651.7 6.7 multiply_reduce_fusion.18
  672.7 5.6 fusion.277
  681.6 6.7 multiply_reduce_fusion.18
  706.9 167.9 %while.59 = (s32[]{:T(128)}, bf16[6,1024,2,64]{1,3,2,0:T(8,128)(2,1)S(1)}, bf16[6,1024,2,64]{1,3,2,0:T(8,128)(2,1)}, bf16[6,1024,2,64]{1,3,2,0:T(8,128)(2,1)S(1)...) while((s32[]{:T(128)}, ...), condition=%wide.region_33.34_spmd.clone, body=%wide.region_31.33_spmd.clone.sunk | while | flops 1374943232 | bytes 95747880 | solution.py:108
  708.6 5.6 fusion.289
  717.5 6.7 multiply_reduce_fusion.19
  736.5 5.6 fusion.289
  745.4 6.7 multiply_reduce_fusion.19
  764.4 5.6 fusion.289
  773.3 6.7 multiply_reduce_fusion.19
  792.3 5.6 fusion.289
  801.2 6.7 multiply_reduce_fusion.19
  820.2 5.6 fusion.289
  829.1 6.7 multiply_reduce_fusion.19
  848.2 5.6 fusion.289
  857.0 6.7 multiply_reduce_fusion.19
  903.7 8.5 fusion.158
  912.2 10.5 convolution_add_fusion
  923.4 9.2 fusion.164
  932.7 11.0 convolution_add_fusion.1
  949.8 40.8 %all-reduce.18 = (f32[768]{0:T(1024)S(1)}, f32[768]{0:T(1024)S(1)}, f32[768]{0:T(1024)S(1)}, f32[768]{0:T(1024)S(1)}, f32[768]{0:T(1024)S(1)}, /*index=5*/f32[30...) all-reduce(f32[768]{0:T(1024)S(1)} %add.382, ...), channel_id=3, replica_groups=mesh['fsdp'=32] {'fsdp'}, use_global_device_ids=true, to_apply=%region_37.38.clone | all-reduce | flops 9216 | bytes 73728
  1014.1 73.5 %reduce-scatter.21.cloned.1.call-done = f32[24,768]{1,0:T(8,128)} async-done(((f32[768,768]{1,0:T(8,128)}), f32[24,768]{1,0:T(8,128)}) %reduce-scatter.21.cloned.1.call-update) | async-done | bytes 73744
  1087.6 104.6 %reduce-scatter.19.cloned.1.call-done = f32[24,768]{1,0:T(8,128)} async-done(((f32[768,768]{1,0:T(8,128)}), f32[24,768]{1,0:T(8,128)}) %reduce-scatter.19.cloned.1.call-update) | async-done | bytes 73744
  1192.3 141.1 %reduce-scatter.17.cloned.1.call-done = f32[96,768]{1,0:T(8,128)} async-done(((f32[3072,768]{1,0:T(8,128)}), f32[96,768]{1,0:T(8,128)}) %reduce-scatter.17.cloned.1.call-update) | async-done | bytes 294928 | tf_op jit(solution)/shard_map/reduce_scatter | solution.py:367
  1333.3 141.9 %reduce-scatter.15.cloned.1.call-done = f32[24,3072]{1,0:T(8,128)} async-done(((f32[768,3072]{1,0:T(8,128)}), f32[24,3072]{1,0:T(8,128)}) %reduce-scatter.15.cloned.1.call-update) | async-done | bytes 294928 | tf_op jit(solution)/shard_map/reduce_scatter | solution.py:365
  (568 shorter events, 444.1 us)
Async XLA Ops:
  7.2 62.5 %all-gather.11.cloned.1.call-start = ((), (), s32[]{:S(2)}) async-start(), calls=%async_computation.8 | async-start | bytes 1216512 | tf_op jit(solution)/shard_map/all_gather | solution.py:319
  7.9 116.0 %all-gather.7.cloned.1.call-start = ((), (), s32[]{:S(2)}) async-start(), calls=%async_computation.6 | async-start | bytes 1216512 | tf_op jit(solution)/shard_map/all_gather | solution.py:320
  8.7 171.2 %all-gather.9.cloned.1.call-start = ((), (), s32[]{:S(2)}) async-start(), calls=%async_computation.7 | async-start | bytes 1216512 | tf_op jit(solution)/shard_map/all_gather | solution.py:317
  9.4 238.6 %all-gather.13.cloned.1.call-start = ((), (), s32[]{:S(2)}) async-start(), calls=%async_computation.9 | async-start | bytes 1216512 | tf_op jit(solution)/shard_map/all_gather | solution.py:322
  10.0 338.9 %all-gather.15.cloned.1.call-start = ((), (), s32[]{:S(2)}) async-start(), calls=%async_computation.10 | async-start | bytes 4866048 | tf_op jit(solution)/shard_map/all_gather | solution.py:326
  10.6 412.0 %all-gather.17.cloned.1.call-start = ((), (), s32[]{:S(2)}) async-start(), calls=%async_computation.11 | async-start | bytes 4866048 | tf_op jit(solution)/shard_map/all_gather | solution.py:328
  11.1 1003.0 %reduce-scatter.13.cloned.1.call-start = ((), (), s32[]{:S(2)}) async-start(), calls=%async_computation.12 | async-start | bytes 2433024 | tf_op jit(solution)/shard_map/reduce_scatter | solution.py:361
  253.7 95.2 %copy-start = (f32[1024,768]{1,0:T(8,128)}, f32[1024,768]{1,0:T(8,128)S(1)}, u32[]{:S(2)}) copy-start(f32[1024,768]{1,0:T(8,128)S(1)} %get-tuple-element.515) | copy-start | bytes 9437188
  253.7 95.2 %copy-start.42 = (f32[1024]{0:T(1024)}, f32[1024]{0:T(1024)S(1)}, u32[]{:S(2)}) copy-start(f32[1024]{0:T(1024)S(1)} %broadcast_multiply_fusion.9) | copy-start | bytes 12292
  255.8 93.1 %copy-start.45 = (f32[1024]{0:T(1024)}, f32[1024]{0:T(1024)S(1)}, u32[]{:S(2)}) copy-start(f32[1024]{0:T(1024)S(1)} %add_rsqrt_fusion.1) | copy-start | bytes 12292
  346.7 143.0 %copy-start.48 = (f32[1024]{0:T(1024)}, f32[1024]{0:T(1024)S(1)}, u32[]{:S(2)}) copy-start(f32[1024]{0:T(1024)S(1)} %broadcast_multiply_fusion.11) | copy-start | bytes 12292
  348.8 140.9 %copy-start.50 = (f32[1024]{0:T(1024)}, f32[1024]{0:T(1024)S(1)}, u32[]{:S(2)}) copy-start(f32[1024]{0:T(1024)S(1)} %add_rsqrt_fusion.3) | copy-start | bytes 12292
  348.8 12.1 copy-start.65
  348.9 12.0 copy-start.6
  348.9 12.0 copy-start.74
  360.9 61.6 %copy-start.7 = (f32[1024,768]{1,0:T(8,128)S(1)}, f32[1024,768]{1,0:T(8,128)}, u32[]{:S(2)}) copy-start(f32[1024,768]{1,0:T(8,128)} %copy-done.5) | copy-start | bytes 9437188
  360.9 61.6 %copy-start.73 = (f32[768]{0:T(1024)S(1)}, f32[768]{0:T(1024)}, u32[]{:S(2)}) copy-start(f32[768]{0:T(1024)} %convert_element_type.284) | copy-start | bytes 9220
  422.5 10.3 slice-start.4
  422.5 10.3 slice-start.6
  422.6 10.3 slice-start.5
  422.6 10.3 slice-start.7
  450.4 14.2 copy-start.27
  450.4 26.8 %copy-start.25 = (f32[1024,768]{1,0:T(8,128)}, f32[1024,768]{1,0:T(8,128)S(1)}, u32[]{:S(2)}) copy-start(f32[1024,768]{1,0:T(8,128)S(1)} %get-tuple-element.484) | copy-start | bytes 9437188
  464.6 12.6 copy-start.11
  489.7 14.6 copy-start.21
  510.1 191.2 %copy-start.3 = (f32[1024,768]{1,0:T(8,128)}, f32[1024,768]{1,0:T(8,128)S(1)}, u32[]{:S(2)}) copy-start(f32[1024,768]{1,0:T(8,128)S(1)} %get-tuple-element.488) | copy-start | bytes 9437188
  512.9 501.2 %reduce-scatter.23.cloned.1.call-start = ((), (), s32[]{:S(2)}) async-start(), calls=%async_computation.17 | async-start | bytes 2433024
  531.9 6.8 slice-start
  531.9 6.8 slice-start.1
  561.9 6.7 slice-start
  562.0 6.7 slice-start.1
  591.9 6.8 slice-start
  591.9 6.8 slice-start.1
  621.8 6.7 slice-start
  681.6 6.7 slice-start
  681.6 6.7 slice-start.1
  829.1 6.7 slice-start.2
  829.1 6.7 slice-start.3
  874.8 22.8 %copy-start.13 = (bf16[6,1024,2,64]{1,3,2,0:T(8,128)(2,1)}, bf16[6,1024,2,64]{1,3,2,0:T(8,128)(2,1)S(1)}, u32[]{:S(2)}) copy-start(bf16[6,1024,2,64]{1,3,2,0:T(8,128)(2,1)S(1)} %get-tuple-element.228) | copy-start | bytes 4718596
  885.5 202.1 %reduce-scatter.21.cloned.1.call-start = ((), (), s32[]{:S(2)}) async-start(), calls=%async_computation.16 | async-start | bytes 2433024
  894.6 297.6 %reduce-scatter.19.cloned.1.call-start = ((), (), s32[]{:S(2)}) async-start(), calls=%async_computation.15 | async-start | bytes 2433024
  903.6 8.5 copy-start.26
  903.6 429.7 %reduce-scatter.17.cloned.1.call-start = ((), (), s32[]{:S(2)}) async-start(), calls=%async_computation.14 | async-start | bytes 9732096 | tf_op jit(solution)/shard_map/reduce_scatter | solution.py:367
  922.7 9.9 copy-start.2
  922.7 9.9 copy-start.44
  922.7 9.9 copy-start.47
  922.7 552.4 %reduce-scatter.15.cloned.1.call-start = ((), (), s32[]{:S(2)}) async-start(), calls=%async_computation.13 | async-start | bytes 9732096 | tf_op jit(solution)/shard_map/reduce_scatter | solution.py:365
  943.9 52.0 %copy-start.12 = (bf16[1024,768]{1,0:T(8,128)(2,1)S(1)}, bf16[1024,768]{1,0:T(8,128)(2,1)}, u32[]{:S(2)}) copy-start(bf16[1024,768]{1,0:T(8,128)(2,1)} %get-tuple-element.500) | copy-start | bytes 4718596
  (86 other events, 319.4 us)
Sparse Core Ops, SparseCore 0:
  10.9 56.9 all-gather.10
  70.8 53.1 all-gather.6
  126.9 52.9 all-gather.8
  182.6 52.9 all-gather.12
  238.3 62.4 all-gather.14
  303.6 62.4 all-gather.16
  513.0 97.9 reduce-scatter.12
  885.6 98.1 reduce-scatter.22
  989.6 97.9 reduce-scatter.20
  1094.2 98.0 reduce-scatter.18
  1198.7 134.5 reduce-scatter.16
  1340.7 134.4 reduce-scatter.14
where the time goes:
time: 1500 us; the launch traced here: 1480 us
  matrix products  585 us (39%)
  waiting for transfers between devices  567 us (38%)
  other arithmetic  104 us (7%)
  blocking collectives  83.2 us (6%)
  local copies, waits for them, and re-layouts  75.5 us (5%)
  loops' own time  51.1 us (3%)
  between operations  15.9 us (1%)
    unnamed x15, waiting for transfers between devices  182 us
    reduce_scatter x1, waiting for transfers between devices, on_device(): lax.psum_scatter(totals[9], 'fsdp', scatter_dimension=0, tiled=True)  142 us
    reduce_scatter x1, waiting for transfers between devices, on_device(): lax.psum_scatter(totals[11], 'fsdp', scatter_dimension=0, tiled=True)  141 us
    dot_general x24, matrix products, pair_scores(): jnp.einsum('qhd,khd->hqk', query_pair, keys_pair, preferred_element_type=...  101 us
    unnamed x2, blocking collectives  83.2 us
    dot_general x12, matrix products, one_pair(): jnp.einsum('qhd,khd->hqk', upstream_pair, values_pair, preferred_element_...  80.6 us
    dot_general x12, matrix products, times_transposed(): jnp.einsum('tj,ij->ti', left, right, preferred_element_type=jnp.float32)  72.9 us
    dot_general x2, matrix products, layer_forward(): jnp.dot(hidden_low, up_weight, preferred_element_type=jnp.float32) + up_bias  69 us
  transfers between devices with their start and end apart: 12, of which 6 were waited for; matrix products, arithmetic and copies ran while one was open for 44% of the time, Pallas kernels for 0%

commit v1 on v0

v1 whole, which is shorter than its diff:
```python
import functools
import math

import jax
import jax.numpy as jnp
from jax import lax
from jax.experimental import pallas as pl
from jax.experimental.pallas import tpu as pltpu
from jax.sharding import PartitionSpec as P

HD = 64
LANES = 128
BLOCK = 256

epsilon = 1e-05
neg_fill = -1e30


def normalize(rows):
    center = rows - jnp.mean(rows, axis=-1, keepdims=True)
    scale = lax.rsqrt(jnp.mean(center * center, axis=-1, keepdims=True) + epsilon)
    return (center * scale, scale)


def norm_back(incoming, normed, scale):
    return scale * (
        incoming
        - jnp.mean(incoming, axis=-1, keepdims=True)
        - normed * jnp.mean(incoming * normed, axis=-1, keepdims=True)
    )


def rows_outer(left, right):
    out = jnp.einsum("ti,tj->ij", left, right, preferred_element_type=jnp.float32)
    return out.astype(jnp.bfloat16)


def times_transposed(left, right):
    return jnp.einsum("tj,ij->ti", left, right, preferred_element_type=jnp.float32)


def nt(left, right):
    return lax.dot_general(
        left, right, (((1,), (1,)), ((), ())), preferred_element_type=jnp.float32
    )


def three_parts(value):
    high = value.astype(jnp.bfloat16).astype(jnp.float32)
    rest = value - high
    middle = rest.astype(jnp.bfloat16).astype(jnp.float32)
    return (high, middle, rest - middle)


def forward_kernel(q_ref, k_ref, v_ref, mq_ref, mk_ref, out_ref, aug_ref):
    length = q_ref.shape[0]
    lane = lax.broadcasted_iota(jnp.int32, (length, LANES), 1)
    low_half = lane < HD
    query = q_ref[...] * jnp.asarray(HD**-0.5, jnp.bfloat16)
    keys, values = k_ref[...], v_ref[...]
    mq, mk = mq_ref[...], mk_ref[...]
    ones = jnp.ones_like(values)
    operands = []
    for head in range(2):
        mine = low_half if head == 0 else jnp.logical_not(low_half)
        operands.append(
            (
                jnp.where(mine, query, mq),
                jnp.where(mine, keys, mk),
                jnp.where(mine, values, ones),
            )
        )
    lane = lane[:BLOCK]
    low_half = low_half[:BLOCK]
    spot = lane % HD
    for start in range(0, length, BLOCK):
        mixed, logs = [], []
        for head in range(2):
            q_aug, k_aug, v_aug = operands[head]
            scores = nt(q_aug[start : start + BLOCK], k_aug)
            top = jnp.max(scores, axis=-1, keepdims=True)
            raised = jnp.exp(scores - top).astype(jnp.bfloat16)
            both = jnp.dot(raised, v_aug, preferred_element_type=jnp.float32)
            mixed.append(both / pltpu.roll(both, HD, 1))
            logs.append((top, both))
        out_ref[start : start + BLOCK, :] = jnp.where(low_half, mixed[0], mixed[1]).astype(
            jnp.bfloat16
        )
        total = jnp.where(low_half, logs[1][1], logs[0][1])
        top = jnp.where(low_half, logs[1][0], logs[0][0])
        high, middle, rest = three_parts(top + jnp.log(total))
        aug = jnp.where(
            spot == 8,
            high,
            jnp.where(
                spot == 9,
                middle,
                jnp.where(spot == 10, rest, mq[start : start + BLOCK].astype(jnp.float32)),
            ),
        )
        aug_ref[start : start + BLOCK, :] = aug.astype(jnp.bfloat16)


def backward_kernel(q_ref, k_ref, v_ref, aug_ref, mk_ref, o_ref, up_ref, dq_ref, dk_ref, dv_ref):
    length = q_ref.shape[0]
    scale = HD**-0.5
    lane = lax.broadcasted_iota(jnp.int32, (length, LANES), 1)
    low_half = lane < HD
    spot = lane % HD
    query = q_ref[...] * jnp.asarray(scale, jnp.bfloat16)
    keys, values, upstream = k_ref[...], v_ref[...], up_ref[...]
    aug, mk = aug_ref[...], mk_ref[...]
    product = upstream.astype(jnp.float32) * o_ref[...].astype(jnp.float32)
    zero = jnp.zeros_like(product)
    inner_low = jnp.sum(jnp.where(low_half, product, zero), axis=-1, keepdims=True)
    inner_high = jnp.sum(jnp.where(low_half, zero, product), axis=-1, keepdims=True)
    high, middle, rest = three_parts(jnp.where(low_half, inner_high, inner_low))
    up_aug = jnp.where(
        spot == 8, high, jnp.where(spot == 9, middle, jnp.where(spot == 10, rest, zero))
    ).astype(jnp.bfloat16)
    minus = jnp.where((spot >= 8) & (spot <= 10), -1.0, zero).astype(jnp.bfloat16)
    keys_turned = keys.astype(jnp.float32).T.astype(jnp.bfloat16)
    operands = []
    for head in range(2):
        mine = low_half if head == 0 else jnp.logical_not(low_half)
        operands.append(
            (
                jnp.where(mine, query, aug),
                jnp.where(mine, keys, mk),
                jnp.where(mine, upstream, up_aug),
                jnp.where(mine, values, minus),
            )
        )
    small_half = low_half[:BLOCK]
    turned = [None, None]
    for start in range(0, length, BLOCK):
        block = slice(start, start + BLOCK)
        key_parts, value_parts = [], []
        for head in range(2):
            q_aug, k_aug, u_aug, v_aug = operands[head]
            shares = jnp.exp(nt(k_aug[block], q_aug))
            score_back = (shares * nt(v_aug[block], u_aug)).astype(jnp.bfloat16)
            value_parts.append(
                jnp.dot(shares.astype(jnp.bfloat16), upstream, preferred_element_type=jnp.float32)
            )
            key_parts.append(jnp.dot(score_back, query, preferred_element_type=jnp.float32))
            part = jnp.dot(
                keys_turned[head * HD : (head + 1) * HD, block],
                score_back,
                preferred_element_type=jnp.float32,
            )
            turned[head] = part if turned[head] is None else turned[head] + part
        dk_ref[block, :] = jnp.where(small_half, key_parts[0], key_parts[1]).astype(jnp.bfloat16)
        dv_ref[block, :] = jnp.where(small_half, value_parts[0], value_parts[1]).astype(
            jnp.bfloat16
        )
    dq_ref[...] = (jnp.concatenate(turned, axis=0).T * scale).astype(jnp.bfloat16)


def attention_specs(length):
    wide = pl.BlockSpec((length, LANES), lambda slot, pair: (slot, pair))
    single = pl.BlockSpec((length, LANES), lambda slot, pair: (slot, 0))
    return wide, single


def attend_forward(query, keys, values, mq, mk, length):
    rows, width = query.shape
    wide, single = attention_specs(length)
    shape = jax.ShapeDtypeStruct((rows, width), jnp.bfloat16)
    return pl.pallas_call(
        forward_kernel,
        grid=(rows // length, width // LANES),
        in_specs=[wide, wide, wide, single, single],
        out_specs=[wide, wide],
        out_shape=[shape, shape],
        compiler_params=pltpu.CompilerParams(vmem_limit_bytes=48 * 2**20),
        cost_estimate=pl.CostEstimate(
            flops=8 * rows * length * width,
            bytes_accessed=10 * rows * width,
            transcendentals=rows * length * width // HD,
        ),
    )(query, keys, values, mq, mk)


def attend_backward(query, keys, values, aug, mk, attended, upstream, length):
    rows, width = query.shape
    wide, single = attention_specs(length)
    shape = jax.ShapeDtypeStruct((rows, width), jnp.bfloat16)
    return pl.pallas_call(
        backward_kernel,
        grid=(rows // length, width // LANES),
        in_specs=[wide, wide, wide, wide, single, wide, wide],
        out_specs=[wide, wide, wide],
        out_shape=[shape, shape, shape],
        compiler_params=pltpu.CompilerParams(vmem_limit_bytes=48 * 2**20),
        cost_estimate=pl.CostEstimate(
            flops=20 * rows * length * width,
            bytes_accessed=18 * rows * width,
            transcendentals=rows * length * width // HD,
        ),
    )(query, keys, values, aug, mk, attended, upstream)


def slot_masks(lengths, length):
    bounds = jnp.cumsum(lengths, axis=1, dtype=jnp.int32)
    places = jnp.arange(length, dtype=jnp.int32)
    past = (places[None, :, None] >= bounds[:, None, :]).astype(jnp.int32)
    labels = jnp.sum(past, axis=2).reshape(-1)
    live = (places[None, :] < bounds[:, -1:]).astype(jnp.float32).reshape(-1)
    spot = jnp.arange(LANES, dtype=jnp.int32)[None, :] % HD
    kinds = lengths.shape[1] + 1
    hit = spot == labels[:, None]
    mq = jnp.where(hit, 1.0, 0.0).astype(jnp.bfloat16)
    mk = jnp.where((spot < kinds) & jnp.logical_not(hit), neg_fill, 0.0)
    mk = jnp.where((spot >= 8) & (spot <= 10), -1.0, mk).astype(jnp.bfloat16)
    return live, mq, mk


def scatter_sum(full, width, order):
    bits = width.bit_length() - 1
    chunk = (full.shape[0] // width,) + full.shape[1:]
    data = full.reshape((2,) * bits + chunk)
    me = lax.axis_index("fsdp")
    axes = list(range(bits - 1, -1, -1))
    for bit in order:
        axis = axes.index(bit)
        axes.pop(axis)
        mine = lax.rem(lax.div(me, 1 << bit), 2)
        send = lax.dynamic_index_in_dim(data, 1 - mine, axis, keepdims=False)
        keep = lax.dynamic_index_in_dim(data, mine, axis, keepdims=False)
        pairs = [(device, device ^ (1 << bit)) for device in range(width)]
        came = lax.ppermute(send, "fsdp", pairs)
        data = (keep.astype(jnp.float32) + came.astype(jnp.float32)).astype(full.dtype)
    return data


def orders(width):
    bits = width.bit_length() - 1
    rest = list(range(1, bits))
    return [[0] + rest[turn:] + rest[:turn] for turn in range(max(1, len(rest)))]


def on_device(
    tokens,
    seq_lengths,
    query_weight,
    query_bias,
    key_weight,
    value_weight,
    value_bias,
    output_weight,
    output_bias,
    first_gain,
    first_shift,
    up_weight,
    up_bias,
    down_weight,
    down_bias,
    second_gain,
    second_shift,
    cotangent,
):
    width = lax.axis_size("fsdp")
    length = tokens.shape[0] // seq_lengths.shape[1]
    model = tokens.shape[1]
    hidden_units = up_weight.shape[1]
    gather = functools.partial(lax.all_gather, axis_name="fsdp", axis=0, tiled=False)

    vectors = (
        query_bias,
        value_bias,
        output_bias,
        first_gain,
        first_shift,
        up_bias,
        down_bias,
        second_gain,
        second_shift,
    )
    sizes = [piece.shape[0] for piece in vectors]
    flat = jnp.concatenate(vectors)
    flat_rows = -(-flat.shape[0] // model)
    flat = jnp.pad(flat, (0, flat_rows * model - flat.shape[0])).reshape(flat_rows, model)
    part = query_weight.shape[0]
    early = gather(jnp.concatenate([query_weight, key_weight, value_weight, flat], axis=0))
    late = gather(
        jnp.concatenate([output_weight, down_weight, up_weight.reshape(-1, model)], axis=0)
    )

    full_vectors = []
    gathered_flat = early[:, 3 * part :].reshape(width, -1)
    start = 0
    for size in sizes:
        full_vectors.append(
            gathered_flat[:, start : start + size].reshape(-1).astype(jnp.float32)
        )
        start += size
    (
        query_bias,
        value_bias,
        output_bias,
        first_gain,
        first_shift,
        up_bias,
        down_bias,
        second_gain,
        second_shift,
    ) = full_vectors
    query_weight = early[:, :part].reshape(model, model)
    key_weight = early[:, part : 2 * part].reshape(model, model)
    value_weight = early[:, 2 * part : 3 * part].reshape(model, model)
    down_part = down_weight.shape[0]
    output_weight = late[:, :part].reshape(model, model)
    down_weight = late[:, part : part + down_part].reshape(hidden_units, model)
    up_weight = late[:, part + down_part :].reshape(model, hidden_units)

    live, mq, mk = slot_masks(seq_lengths[0], length)
    live = live[:, None]
    query = (jnp.dot(tokens, query_weight, preferred_element_type=jnp.float32) + query_bias).astype(
        jnp.bfloat16
    )
    keys = jnp.dot(tokens, key_weight, preferred_element_type=jnp.float32).astype(jnp.bfloat16)
    values = (
        jnp.dot(tokens, value_weight, preferred_element_type=jnp.float32) + value_bias
    ).astype(jnp.bfloat16)
    attended, aug = attend_forward(query, keys, values, mq, mk, length)
    first = (
        tokens.astype(jnp.float32)
        + jnp.dot(attended, output_weight, preferred_element_type=jnp.float32)
        + output_bias
    )
    normed_one, scale_one = normalize(first)
    hidden = normed_one * first_gain + first_shift
    hidden_low = hidden.astype(jnp.bfloat16)
    upward = jnp.dot(hidden_low, up_weight, preferred_element_type=jnp.float32) + up_bias
    share = 0.5 * (1.0 + lax.erf(upward * (1.0 / math.sqrt(2.0))))
    active = (upward * share).astype(jnp.bfloat16)
    slope = (
        share + upward * jnp.exp(-0.5 * upward * upward) * (1.0 / math.sqrt(2.0 * math.pi))
    ).astype(jnp.bfloat16)
    second = hidden + jnp.dot(active, down_weight, preferred_element_type=jnp.float32) + down_bias
    normed_two, scale_two = normalize(second)
    layer_output = ((normed_two * second_gain + second_shift) * live).astype(jnp.bfloat16)

    upstream = cotangent.astype(jnp.float32) * live
    second_shift_back = jnp.sum(upstream, axis=0)
    second_gain_back = jnp.sum(upstream * normed_two, axis=0)
    second_back = norm_back(upstream * second_gain, normed_two, scale_two)
    mix_low = second_back.astype(jnp.bfloat16)
    ways = orders(width)
    down_weight_back = scatter_sum(rows_outer(active, mix_low), width, ways[0])
    down_bias_back = jnp.sum(mix_low.astype(jnp.float32), axis=0)
    up_low = (times_transposed(mix_low, down_weight) * slope).astype(jnp.bfloat16)
    up_weight_back = scatter_sum(rows_outer(hidden_low, up_low), width, ways[1 % len(ways)])
    up_bias_back = jnp.sum(up_low.astype(jnp.float32), axis=0)
    hidden_back = second_back + times_transposed(up_low, up_weight)
    first_shift_back = jnp.sum(hidden_back, axis=0)
    first_gain_back = jnp.sum(hidden_back * normed_one, axis=0)
    first_back = norm_back(hidden_back * first_gain, normed_one, scale_one)
    out_low = first_back.astype(jnp.bfloat16)
    output_weight_back = scatter_sum(rows_outer(attended, out_low), width, ways[2 % len(ways)])
    output_bias_back = jnp.sum(out_low.astype(jnp.float32), axis=0)
    attended_back = times_transposed(out_low, output_weight).astype(jnp.bfloat16)
    query_low, key_low, value_low = attend_backward(
        query, keys, values, aug, mk, attended, attended_back, length
    )
    query_weight_back = scatter_sum(rows_outer(tokens, query_low), width, ways[0])
    key_weight_back = scatter_sum(rows_outer(tokens, key_low), width, ways[1 % len(ways)])
    value_weight_back = scatter_sum(rows_outer(tokens, value_low), width, ways[2 % len(ways)])
    query_bias_back = jnp.sum(query_low.astype(jnp.float32), axis=0)
    value_bias_back = jnp.sum(value_low.astype(jnp.float32), axis=0)
    token_gradient = (
        first_back
        + times_transposed(query_low, query_weight)
        + times_transposed(key_low, key_weight)
        + times_transposed(value_low, value_weight)
    )
    vector_backs = (
        query_bias_back,
        value_bias_back,
        output_bias_back,
        first_gain_back,
        first_shift_back,
        up_bias_back,
        down_bias_back,
        second_gain_back,
        second_shift_back,
    )
    packed = jnp.concatenate([piece.reshape(width, -1) for piece in vector_backs], axis=1)
    summed = scatter_sum(packed, width, ways[0]).reshape(-1)
    split = []
    start = 0
    for size in sizes:
        split.append(summed[start : start + size])
        start += size
    (
        query_bias_back,
        value_bias_back,
        output_bias_back,
        first_gain_back,
        first_shift_back,
        up_bias_back,
        down_bias_back,
        second_gain_back,
        second_shift_back,
    ) = split
    return (
        layer_output,
        token_gradient,
        query_weight_back.astype(jnp.float32),
        query_bias_back,
        key_weight_back.astype(jnp.float32),
        value_weight_back.astype(jnp.float32),
        value_bias_back,
        output_weight_back.astype(jnp.float32),
        output_bias_back,
        first_gain_back,
        first_shift_back,
        up_weight_back.astype(jnp.float32),
        up_bias_back,
        down_weight_back.astype(jnp.float32),
        down_bias_back,
        second_gain_back,
        second_shift_back,
    )


def solution(mesh):
    rows, flat = P("fsdp", None), P("fsdp")
    return jax.shard_map(
        on_device,
        mesh=mesh,
        in_specs=(
            rows,
            P("fsdp", None, None),
            rows,
            flat,
            rows,
            rows,
            flat,
            rows,
            flat,
            flat,
            flat,
            rows,
            flat,
            rows,
            flat,
            flat,
            flat,
            rows,
        ),
        out_specs=(
            rows,
            rows,
            rows,
            flat,
            rows,
            rows,
            flat,
            rows,
            flat,
            flat,
            flat,
            rows,
            flat,
            rows,
            flat,
            flat,
            flat,
        ),
        check_vma=False,
    )
```

time: 1500 us -> 614 us (0.41)
  waiting for transfers between devices: 567 us -> 149 us
  matrix products: 585 us -> 174 us
  Pallas kernels: 0 us -> 123 us
  blocking collectives: 83.2 us -> 0 us
  other arithmetic: 104 us -> 42 us
  loops' own time: 51.1 us -> 0 us
  starting transfers between devices: 0.47 us -> 30.8 us
    dot_general x96 -> x6, matrix products: 447 us -> 54.9 us  [the longest x1 21.4 us: on_device(): jnp.dot(hidden_low, up_weight, preferred_element_type=jnp.float32) + up_bias]
    reduce_scatter x3 -> x0, waiting for transfers between devices: 283 us -> none  [the longest x1 142 us: on_device(): lax.psum_scatter(totals[9], 'fsdp', scatter_dimension=0, tiled=True)]
    unnamed x15 -> x2, waiting for transfers between devices: 182 us -> 0.03 us
    pallas_call x0 -> x2, Pallas kernels: none -> 123 us  [the longest x1 72.7 us: attend_backward(): pl.pallas_call(backward_kernel, grid=(rows // length, width // LANES), in...]
    unnamed x2 -> x0, blocking collectives: 83.2 us -> none
    ppermute x0 -> x35, waiting for transfers between devices: none -> 77.3 us  [scatter_sum(): came = lax.ppermute(send, 'fsdp', pairs)]
    another operation x4 -> x0, loops' own time: 51.1 us -> none  [the longest x2 32.7 us: attend_backward(): return lax.map(one_pair, jnp.arange(query.shape[1] // 2, dtype=jnp.int32))]
    all_gather x6 -> x2, waiting for transfers between devices: 103 us -> 71.3 us  [the longest x1 51.9 us: on_device(): gather(jnp.concatenate([query_weight, key_weight, value_weight, flat], ax...]
  transfers between devices with their start and end apart: 12 -> 37, of which waited for: 6 -> 19; matrix products, arithmetic and copies ran while one was open for 44% -> 13% of each run, Pallas kernels for 0% -> 8%
where the time goes in v1:
time: 614 us; the launch traced here: 607 us
  matrix products  174 us (28%)
  waiting for transfers between devices  149 us (24%)
  Pallas kernels  123 us (20%)
  local copies, waits for them, and re-layouts  72.7 us (12%)
  other arithmetic  42 us (7%)
  starting transfers between devices  30.8 us (5%)
  between operations  15.3 us (2%)
    ppermute x35, waiting for transfers between devices, scatter_sum(): came = lax.ppermute(send, 'fsdp', pairs)  77.3 us
    pallas_call x1, Pallas kernels, attend_backward(): pl.pallas_call(backward_kernel, grid=(rows // length, width // LANES), in...  72.7 us
    dot_general x6, matrix products, times_transposed(): jnp.einsum('tj,ij->ti', left, right, preferred_element_type=jnp.float32)  71.6 us
    all_gather x1, waiting for transfers between devices, on_device(): gather(jnp.concatenate([query_weight, key_weight, value_weight, flat], ax...  51.9 us
    pallas_call x1, Pallas kernels, attend_forward(): pl.pallas_call(forward_kernel, grid=(rows // length, width // LANES), in_...  50.7 us
    dot_general x6, matrix products, rows_outer(): jnp.einsum('ti,tj->ij', left, right, preferred_element_type=jnp.float32)  47.3 us
    ppermute x35, starting transfers between devices, scatter_sum(): came = lax.ppermute(send, 'fsdp', pairs)  30.7 us
    unnamed x85, local copies, waits for them, and re-layouts  23.3 us
  transfers between devices with their start and end apart: 37, of which 19 were waited for; matrix products, arithmetic and copies ran while one was open for 13% of the time, Pallas kernels for 8%

profile of v1, /device:TPU:0, one launch (start us, length us, event | category | flops | bytes accessed | tf_op | source)
XLA Modules:
  0.0 606.7 jit_solution(5675034096346985781)
XLA Ops:
  7.2 6.3 %concatenate.31 = bf16[288]{0:T(512)(128)(2,1)S(1)} concatenate(bf16[24]{0:T(256)(128)(2,1)} %param.21, bf16[24]{0:T(256)(128)(2,1)} %param.24, bf16[24]{0:T(256)(128)(2,1)} %param.26, bf16[24]{0:T(256)(128)(2,1)} %param.27, bf16[24]{0:T(256)(128)(2,1)} %param.28, bf16[96]{0:T(256)(128)(2,1)} %param.30, bf16[24]{0:T(256)(128)(2,1)} %param.32, bf16[24]{0:T(256)(128)(2,1)} %param.33, ...), dimensions={0} | concatenate | bytes 1152 | tf_op jit(solution)/shard_map/concatenate | solution.py:281
  18.9 4.6 copy.132
  23.8 2.9 copy.138
  27.2 51.9 %all-gather.8.cloned.1.call-done = bf16[32,73,768]{2,1,0:T(8,128)(2,1)} async-done(((bf16[1,73,768]{2,1,0:T(8,128)(2,1)}), bf16[32,73,768]{2,1,0:T(8,128)(2,1)}) %all-gather.8.cloned.1.call-update) | async-done | bytes 3588112 | tf_op jit(solution)/shard_map/all_gather | solution.py:285
  81.1 2.4 fusion.71
  84.1 3.9 fusion.11.k_ref
  88.0 4.0 fusion.12.q_ref
  92.0 4.0 fusion.13.v_ref
  96.0 50.7 %shard_map.305 = (bf16[2048,768]{1,0:T(8,128)(2,1)S(1)}, bf16[2048,768]{1,0:T(8,128)(2,1)}) custom-call(bf16[2048,768]{1,0:T(8,128)(2,1)} %fusion.12.q_ref, bf16[2048,768]{1,0:T(8,128)(2,1)} %fusion.11.k_ref, bf16[2048,768]{1,0:T(8,128)(2,1)} %fusion.13.v_ref, bf16[2048,128]{1,0:T(8,128)(2,1)S(1)} %get-tuple-element.151.mq_ref, ...), custom_call_target="tpu_custom_call" | custom-call | flops 12884901888 | bytes 15728640 | tf_op jit(solution)/shard_map/pallas_call | solution.py:170
  148.5 19.4 %all-gather.6.cloned.1.call-done = bf16[6912,768]{1,0:T(8,128)(2,1)} async-done(((bf16[216,768]{1,0:T(8,128)(2,1)}), bf16[6912,768]{1,0:T(8,128)(2,1)}) %all-gather.6.cloned.1.call-update) | async-done | bytes 10616848 | tf_op jit(solution)/shard_map/all_gather | solution.py:286
  169.2 8.4 %fusion.70 = (bf16[32,96,768]{2,1,0:T(8,128)(2,1)}, bf16[32,96,768]{2,1,0:T(8,128)(2,1)}) fusion(bf16[32,216,768]{2,1,0:T(8,128)(2,1)} %bitcast.288), kind=kLoop, calls=%fused_computation.233 | loop fusion | bytes 18874368 | tf_op jit(solution)/shard_map/slice | solution.py:314
  177.7 3.3 fusion.72
  181.0 2.7 copy-done.7
  184.4 8.5 %reshape.340 = bf16[768,3072]{1,0:T(8,128)(2,1)} reshape(bf16[32,96,768]{2,1,0:T(8,128)(2,1)} %get-tuple-element.125) | data formatting | bytes 9437184 | tf_op jit(solution)/shard_map/reshape | solution.py:315
  192.9 21.4 %multiply_convert_fusion.1 = (bf16[2048,3072]{1,0:T(8,128)(2,1)}, f32[2048,3072]{1,0:T(8,128)}) fusion(f32[3072]{0:T(1024)S(1)} %reshape.353, bf16[768,3072]{1,0:T(8,128)(2,1)} %reshape.340, f32[2048,768]{0,1:T(8,128)} %copy-done.7, f32[768]{0:T(1024)S(1)} %reshape.352, f32[768]{0:T(1024)S(1)} %reshape.351, f32[2048]{0:T(1024)S(1)} %add_rsqrt_fusion.1, ...), kind=kOutput, calls=%fused_computation.8 | convolution fusion | flops 9709289472 | bytes 48793600 | tf_op jit(solution)/shard_map/dot_general | solution.py:335
  214.2 18.4 %fusion.73 = (f32[2048]{0:T(1024)S(1)}, f32[2048,768]{0,1:T(8,128)}) fusion(f32[768]{0:T(1024)S(1)} %reshape.354, bf16[2048,3072]{1,0:T(8,128)(2,1)} %get-tuple-element.162, bf16[3072,768]{1,0:T(8,128)(2,1)} %bitcast.297, f32[768]{0:T(1024)S(1)} %reshape.352, f32[768]{0:T(1024)S(1)} %reshape.351, f32[2048]{0:T(1024)S(1)} %add_rsqrt_fusion.1, ...), kind=kOutput, calls=%fused_computation.236 | convolution fusion | flops 9674684416 | bytes 29918208 | tf_op jit(solution)/shard_map/dot_general | solution.py:341
  232.6 3.6 multiply_reduce_fusion.4
  237.2 5.9 multiply_reduce_fusion
  243.1 6.1 convert_reduce_fusion.1
  249.2 15.7 %convolution_convert_fusion = bf16[3072,768]{1,0:T(8,128)(2,1)} fusion(bf16[2048,3072]{1,0:T(8,128)(2,1)} %get-tuple-element.162, bf16[2048,768]{0,1:T(8,128)(2,1)} %get-tuple-element.121), kind=kOutput, calls=%fused_computation.37 | convolution fusion | flops 9666035712 | bytes 20447232 | tf_op jit(solution)/shard_map/ti,tj->ij/dot_general | solution.py:34
  264.9 26.3 %convert_reduce_fusion = (f32[3072]{0:T(1024)S(1)}, bf16[2048,3072]{1,0:T(8,128)(2,1)}) fusion(f32[2048,3072]{1,0:T(8,128)} %get-tuple-element.163, f32[3072]{0:T(1024)S(1)} %reshape.353, bf16[2048,768]{0,1:T(8,128)(2,1)} %get-tuple-element.121, bf16[3072,768]{1,0:T(8,128)(2,1)S(1)} %bitcast.300), kind=kOutput, calls=%fused_computation.6 | convolution fusion | flops 9758045184 | bytes 45637632 | tf_op jit(solution)/shard_map/tj,ij->ti/dot_general | solution.py:39
  291.2 14.6 %convolution_convert_fusion.1 = bf16[768,3072]{1,0:T(8,128)(2,1)} fusion(bf16[2048,3072]{1,0:T(8,128)(2,1)} %get-tuple-element.168, f32[2048,768]{0,1:T(8,128)S(1)} %bitcast.286, f32[768]{0:T(1024)S(1)} %reshape.352, f32[768]{0:T(1024)S(1)} %reshape.351, f32[2048]{0:T(1024)S(1)} %add_rsqrt_fusion.1, f32[2048]{0:T(1024)S(1)} %broadcast_multiply_fusion.5), kind=kOutput, calls=%fused_computation.38 | convolution fusion | flops 9673900032 | bytes 23615488 | tf_op jit(solution)/shard_map/ti,tj->ij/dot_general | solution.py:34
  305.8 21.8 %multiply_reduce_fusion.1 = (f32[768]{0:T(1024)S(1)}, f32[2048]{0:T(1024)S(1)}, f32[2048]{0:T(1024)S(1)}, f32[768]{0:T(1024)S(1)}, f32[2048,768]{0,1:T(8,128)}) fusion(f32[2048,768]{0,1:T(8,128)} %copy-done.7, f32[2048]{0:T(1024)S(1)} %add_rsqrt_fusion.1, f32[2048]{0:T(1024)S(1)} %broadcast_multiply_fusion.5, f32[768]{0:T(1024)S(1)} %reshape.351, ...), kind=kOutput, calls=%fused_computation.12 | convolution fusion | flops 9693554688 | bytes 39407616 | tf_op jit(solution)/shard_map/tj,ij->ti/dot_general | solution.py:39
  327.6 5.9 convert_reduce_fusion.2
  333.6 3.7 convolution_convert_fusion.4
  337.3 4.1 convolution_convert_fusion.3.up_ref
  341.4 72.7 %shard_map.306 = (bf16[2048,768]{1,0:T(8,128)(2,1)S(1)}, bf16[2048,768]{1,0:T(8,128)(2,1)}, bf16[2048,768]{1,0:T(8,128)(2,1)}) custom-call(bf16[2048,768]{1,0:T(8,128)(2,1)} %fusion.12.q_ref, bf16[2048,768]{1,0:T(8,128)(2,1)} %fusion.11.k_ref, bf16[2048,768]{1,0:T(8,128)(2,1)} %fusion.13.v_ref, bf16[2048,768]{1,0:T(8,128)(2,1)} %get-tuple-element.23.aug_ref, ...), custom_call_target="tpu_custom_call" | custom-call | flops 32212254720 | bytes 28311552 | tf_op jit(solution)/shard_map/pallas_call | solution.py:189
  414.2 5.7 convolution_convert_fusion.5
  420.9 3.7 convolution_convert_fusion.7
  424.6 4.8 fusion.74
  429.4 3.8 convolution_convert_fusion.6
  433.2 4.5 fusion.75
  455.4 10.2 %add_add_fusion = f32[2048,768]{0,1:T(8,128)} fusion(f32[2048,768]{0,1:T(8,128)} %fusion.75, f32[2048,768]{0,1:T(8,128)} %copy-done.4, f32[2048,768]{0,1:T(8,128)} %fusion.74, bf16[2048,768]{1,0:T(8,128)(2,1)S(1)} %copy-done.6, bf16[768,768]{1,0:T(8,128)(2,1)S(1)} %bitcast.290), kind=kOutput, calls=%fused_computation.16 | convolution fusion | flops 2420637696 | bytes 29491200 | tf_op jit(solution)/shard_map/tj,ij->ti/dot_general | solution.py:39
  473.8 6.7 %copy.156 = f32[2048,768]{1,0:T(8,128)} copy(f32[2048,768]{0,1:T(8,128)} %add_add_fusion) | data formatting | bytes 12582912
  480.5 3.0 copy.155
  492.0 4.6 collective-permute-done.21
  498.1 4.0 collective-permute-done.16
  506.0 8.4 %collective-permute-done.22 = bf16[2,2,24,768]{3,2,0,1:T(8,128)(2,1)S(1)} collective-permute-done((bf16[2,2,24,768]{3,2,0,1:T(8,128)(2,1)S(1)}, bf16[2,2,24,768]{3,2,0,1:T(8,128)(2,1)S(1)}, u32[]{:S(2)}, u32[]{:S(2)}) %collective-permute-start.22) | collective-permute-done | bytes 147488 | tf_op jit(solution)/shard_map/ppermute | solution.py:232
  519.9 2.4 collective-permute-done.23
  528.0 2.5 fusion.9
  531.4 2.6 fusion.10
  538.0 18.1 %collective-permute-done.31 = bf16[2,2,2,96,768]{4,3,0,1,2:T(8,128)(2,1)S(1)} collective-permute-done((bf16[2,2,2,96,768]{4,3,0,1,2:T(8,128)(2,1)S(1)}, bf16[2,2,2,96,768]{4,3,0,1,2:T(8,128)(2,1)S(1)}, u32[]{:S(2)}, u32[]{:S(2)}) %collective-permute-start.31) | collective-permute-done | bytes 1179680 | tf_op jit(solution)/shard_map/ppermute | solution.py:232
  557.8 4.5 collective-permute-done.26
  564.0 7.7 %collective-permute-done.32 = bf16[2,2,96,768]{3,2,0,1:T(8,128)(2,1)S(1)} collective-permute-done((bf16[2,2,96,768]{3,2,0,1:T(8,128)(2,1)S(1)}, bf16[2,2,96,768]{3,2,0,1:T(8,128)(2,1)S(1)}, u32[]{:S(2)}, u32[]{:S(2)}) %collective-permute-start.32) | collective-permute-done | bytes 589856 | tf_op jit(solution)/shard_map/ppermute | solution.py:232
  572.6 4.5 collective-permute-done.27
  577.5 5.1 collective-permute-done.33
  583.3 10.3 %collective-permute-done.28 = bf16[2,24,3072]{2,1,0:T(8,128)(2,1)S(1)} collective-permute-done((bf16[2,24,3072]{2,1,0:T(8,128)(2,1)S(1)}, bf16[2,24,3072]{2,1,0:T(8,128)(2,1)S(1)}, u32[]{:S(2)}, u32[]{:S(2)}) %collective-permute-start.28) | collective-permute-done | bytes 294944 | tf_op jit(solution)/shard_map/ppermute | solution.py:232
  596.3 2.5 collective-permute-done.29
  (269 shorter events, 78.6 us)
Async XLA Ops:
  7.2 16.6 %copy-start.13 = (bf16[2048,768]{1,0:T(8,128)(2,1)S(1)}, bf16[2048,768]{1,0:T(8,128)(2,1)}, u32[]{:S(2)}) copy-start(bf16[2048,768]{1,0:T(8,128)(2,1)} %param.35) | copy-start | bytes 9437188
  7.2 71.9 %all-gather.8.cloned.1.call-start = ((), (), s32[]{:S(2)}) async-start(), calls=%async_computation.1 | async-start | bytes 4055040 | tf_op jit(solution)/shard_map/all_gather | solution.py:285
  15.1 152.8 %all-gather.6.cloned.1.call-start = ((), (), s32[]{:S(2)}) async-start(), calls=%async_computation | async-start | bytes 10948608 | tf_op jit(solution)/shard_map/all_gather | solution.py:286
  243.1 21.8 %slice-start.6 = ((s8[4718592]{0:T(1024)(128)(4,1)}), s8[4194304]{0:T(1024)(128)(4,1)S(1)}, s32[]{:S(2)}) async-start(s8[4718592]{0:T(1024)(128)(4,1)} %bitcast.298), calls=%async_computation.8 | async-start | bytes 8388608
  249.2 15.7 %slice-start.7 = ((s8[4718592]{0:T(1024)(128)(4,1)}), s8[524288]{0:T(1024)(128)(4,1)S(1)}, s32[]{:S(2)}) async-start(s8[4718592]{0:T(1024)(128)(4,1)} %bitcast.298), calls=%async_computation.9 | async-start | bytes 1048576
  249.2 42.0 %slice-start = ((s8[6291456]{0:T(1024)(128)(4,1)}), s8[4194304]{0:T(1024)(128)(4,1)S(1)}, s32[]{:S(2)}) async-start(s8[6291456]{0:T(1024)(128)(4,1)} %bitcast.285), calls=%async_computation.2 | async-start | bytes 8388608
  264.9 26.3 %slice-start.1 = ((s8[6291456]{0:T(1024)(128)(4,1)}), s8[2097152]{0:T(1024)(128)(4,1)S(1)}, s32[]{:S(2)}) async-start(s8[6291456]{0:T(1024)(128)(4,1)} %bitcast.285), calls=%async_computation.3 | async-start | bytes 4194304
  341.4 72.7 %copy-start.15 = (bf16[2048,768]{1,0:T(8,128)(2,1)S(1)}, bf16[2048,768]{1,0:T(8,128)(2,1)}, u32[]{:S(2)}) copy-start(bf16[2048,768]{1,0:T(8,128)(2,1)} %param.18) | copy-start | bytes 9437188
  429.4 11.9 %slice-start.4 = ((s8[4718592]{0:T(1024)(128)(4,1)}), s8[4194304]{0:T(1024)(128)(4,1)S(1)}, s32[]{:S(2)}) async-start(s8[4718592]{0:T(1024)(128)(4,1)} %bitcast.294), calls=%async_computation.6 | async-start | bytes 8388608
  441.0 86.9 %collective-permute-start.30 = (bf16[2,2,2,2,96,768]{5,4,0,1,2,3:T(8,128)(2,1)}, bf16[2,2,2,2,96,768]{5,4,0,1,2,3:T(8,128)(2,1)}, u32[]{:S(2)}, u32[]{:S(2)}) collective-permute-start(bf16[2,2,2,2,96,768]{5,4,0,1,2,3:T(8,128)(2,1)} %bitcast.276), channel_id=1, source_target_pairs={{0,1},{1,0},{2,3},{3,2},{4,5},{5,4},{6,7},{7,6},{8,9},{9,8},{10,11... | collective-permute-start | bytes 7077896 | tf_op jit(solution)/shard_map/ppermute | solution.py:232
  444.7 86.7 %collective-permute-start.25 = (bf16[2,2,2,2,24,3072]{5,4,3,0,1,2:T(8,128)(2,1)}, bf16[2,2,2,2,24,3072]{5,4,3,0,1,2:T(8,128)(2,1)}, u32[]{:S(2)}, u32[]{:S(2)}) collective-permute-start(bf16[2,2,2,2,24,3072]{5,4,3,0,1,2:T(8,128)(2,1)} %bitcast.277), channel_id=1, source_target_pairs={{0,1},{1,0},{2,3},{3,2},{4,5},{5,4},{6,7},{7,6},{8,9},{9,8},{10,11... | collective-permute-start | bytes 7077896 | tf_op jit(solution)/shard_map/ppermute | solution.py:232
  446.3 9.1 %copy-start.12 = (bf16[32,24,768]{2,1,0:T(8,128)(2,1)S(1)}, bf16[32,24,768]{2,1,0:T(8,128)(2,1)}, u32[]{:S(2)}) copy-start(bf16[32,24,768]{2,1,0:T(8,128)(2,1)} %copy-done.11) | copy-start | bytes 3538948
  446.3 3.6 collective-permute-start.5
  449.7 35.1 %collective-permute-start.20 = (bf16[2,2,2,2,24,768]{5,4,2,3,0,1:T(8,128)(2,1)}, bf16[2,2,2,2,24,768]{5,4,2,3,0,1:T(8,128)(2,1)}, u32[]{:S(2)}, u32[]{:S(2)}) collective-permute-start(bf16[2,2,2,2,24,768]{5,4,2,3,0,1:T(8,128)(2,1)} %bitcast.278), channel_id=1, source_target_pairs={{0,1},{1,0},{2,3},{3,2},{4,5},{5,4},{6,7},{7,6},{8,9},{9,8},{10,11... | collective-permute-start | bytes 1769480 | tf_op jit(solution)/shard_map/ppermute | solution.py:232
  450.0 4.5 collective-permute-start.6
  454.5 32.2 %collective-permute-start.15 = (bf16[2,2,2,2,24,768]{5,4,2,3,0,1:T(8,128)(2,1)}, bf16[2,2,2,2,24,768]{5,4,2,3,0,1:T(8,128)(2,1)}, u32[]{:S(2)}, u32[]{:S(2)}) collective-permute-start(bf16[2,2,2,2,24,768]{5,4,2,3,0,1:T(8,128)(2,1)} %bitcast.279), channel_id=1, source_target_pairs={{0,1},{1,0},{2,3},{3,2},{4,5},{5,4},{6,7},{7,6},{8,9},{9,8},{10,11... | collective-permute-start | bytes 1769480 | tf_op jit(solution)/shard_map/ppermute | solution.py:232
  454.6 12.4 %copy-start.24 = (bf16[768,768]{0,1:T(8,128)(2,1)S(1)}, bf16[768,768]{0,1:T(8,128)(2,1)}, u32[]{:S(2)}) copy-start(bf16[768,768]{0,1:T(8,128)(2,1)} %convolution_convert_fusion.6) | copy-start | bytes 3538948
  454.6 16.6 %copy-start.23 = (bf16[768,768]{0,1:T(8,128)(2,1)S(1)}, bf16[768,768]{0,1:T(8,128)(2,1)}, u32[]{:S(2)}) copy-start(bf16[768,768]{0,1:T(8,128)(2,1)} %convolution_convert_fusion.7) | copy-start | bytes 3538948
  454.6 11.0 %collective-permute-start.7 = (f32[2,2,1,288]{3,2,1,0:T(1,128)S(1)}, f32[2,2,1,288]{3,2,1,0:T(1,128)S(1)}, u32[]{:S(2)}, u32[]{:S(2)}) collective-permute-start(f32[2,2,1,288]{3,2,1,0:T(1,128)S(1)} %fusion.57), channel_id=1, source_target_pairs={{0,4},{1,5},{2,6},{3,7},{4,0},{5,1},{6,2},{7,3},{8,12},{9,13},{10,... | collective-permute-start | bytes 13832 | tf_op jit(solution)/shard_map/ppermute | solution.py:232
  465.6 3.7 collective-permute-start.8
  469.2 14.2 %collective-permute-start.9 = (f32[1,288]{1,0:T(1,128)S(1)}, f32[1,288]{1,0:T(1,128)S(1)}, u32[]{:S(2)}, u32[]{:S(2)}) collective-permute-start(f32[1,288]{1,0:T(1,128)S(1)} %fusion.63), channel_id=1, source_target_pairs={{0,16},{1,17},{2,18},{3,19},{4,20},{5,21},{6,22},{7,23},{8,24},{9,... | collective-permute-start | bytes 3464 | tf_op jit(solution)/shard_map/ppermute | solution.py:232
  483.5 5.2 collective-permute-start.10
  484.8 5.7 collective-permute-start
  486.7 9.9 %collective-permute-start.21 = (bf16[2,2,2,24,768]{4,3,1,2,0:T(8,128)(2,1)S(1)}, bf16[2,2,2,24,768]{4,3,1,2,0:T(8,128)(2,1)S(1)}, u32[]{:S(2)}, u32[]{:S(2)}) collective-permute-start(bf16[2,2,2,24,768]{4,3,1,2,0:T(8,128)(2,1)S(1)} %dynamic-slice_bitcast_fusion.6), channel_id=1, source_target_pairs={{0,8},{1,9},{2,10},{3,11},{4,12},{5,13},{6,14},{7,15},{8,0},{9,1},... | collective-permute-start | bytes 884744 | tf_op jit(solution)/shard_map/ppermute | solution.py:232
  488.7 13.3 %collective-permute-start.16 = (bf16[2,2,2,24,768]{4,3,1,2,0:T(8,128)(2,1)S(1)}, bf16[2,2,2,24,768]{4,3,1,2,0:T(8,128)(2,1)S(1)}, u32[]{:S(2)}, u32[]{:S(2)}) collective-permute-start(bf16[2,2,2,24,768]{4,3,1,2,0:T(8,128)(2,1)S(1)} %dynamic-slice_bitcast_fusion.7), channel_id=1, source_target_pairs={{0,8},{1,9},{2,10},{3,11},{4,12},{5,13},{6,14},{7,15},{8,0},{9,1},... | collective-permute-start | bytes 884744 | tf_op jit(solution)/shard_map/ppermute | solution.py:232
  490.5 12.8 %collective-permute-start.11 = (bf16[2,2,2,24,768]{4,3,2,0,1:T(8,128)(2,1)S(1)}, bf16[2,2,2,24,768]{4,3,2,0,1:T(8,128)(2,1)S(1)}, u32[]{:S(2)}, u32[]{:S(2)}) collective-permute-start(bf16[2,2,2,24,768]{4,3,2,0,1:T(8,128)(2,1)S(1)} %dynamic-slice_bitcast_fusion.8), channel_id=1, source_target_pairs={{0,4},{1,5},{2,6},{3,7},{4,0},{5,1},{6,2},{7,3},{8,12},{9,13},{10,... | collective-permute-start | bytes 884744 | tf_op jit(solution)/shard_map/ppermute | solution.py:232
  491.9 36.0 %copy-start.10 = (bf16[2,2,2,2,1,96,768]{6,5,4,3,2,1,0:T(8,128)(2,1)S(1)}, bf16[2,2,2,2,1,96,768]{6,5,4,3,2,1,0:T(8,128)(2,1)}, u32[]{:S(2)}) copy-start(bf16[2,2,2,2,1,96,768]{6,5,4,3,2,1,0:T(8,128)(2,1)} %get-tuple-element.127) | copy-start | bytes 7077892
  496.6 8.6 %collective-permute-start.1 = (bf16[2,2,2,24,768]{4,3,0,1,2:T(8,128)(2,1)S(1)}, bf16[2,2,2,24,768]{4,3,0,1,2:T(8,128)(2,1)S(1)}, u32[]{:S(2)}, u32[]{:S(2)}) collective-permute-start(bf16[2,2,2,24,768]{4,3,0,1,2:T(8,128)(2,1)S(1)} %dynamic-slice_bitcast_fusion.9), channel_id=1, source_target_pairs={{0,2},{1,3},{2,0},{3,1},{4,6},{5,7},{6,4},{7,5},{8,10},{9,11},{10,... | collective-permute-start | bytes 884744 | tf_op jit(solution)/shard_map/ppermute | solution.py:232
  502.0 12.3 %collective-permute-start.22 = (bf16[2,2,24,768]{3,2,0,1:T(8,128)(2,1)S(1)}, bf16[2,2,24,768]{3,2,0,1:T(8,128)(2,1)S(1)}, u32[]{:S(2)}, u32[]{:S(2)}) collective-permute-start(bf16[2,2,24,768]{3,2,0,1:T(8,128)(2,1)S(1)} %dynamic-slice_bitcast_fusion.12), channel_id=1, source_target_pairs={{0,16},{1,17},{2,18},{3,19},{4,20},{5,21},{6,22},{7,23},{8,24},{9,... | collective-permute-start | bytes 442376 | tf_op jit(solution)/shard_map/ppermute | solution.py:232
  503.2 14.1 %collective-permute-start.17 = (bf16[2,2,24,768]{3,2,0,1:T(8,128)(2,1)S(1)}, bf16[2,2,24,768]{3,2,0,1:T(8,128)(2,1)S(1)}, u32[]{:S(2)}, u32[]{:S(2)}) collective-permute-start(bf16[2,2,24,768]{3,2,0,1:T(8,128)(2,1)S(1)} %dynamic-slice_bitcast_fusion.13), channel_id=1, source_target_pairs={{0,16},{1,17},{2,18},{3,19},{4,20},{5,21},{6,22},{7,23},{8,24},{9,... | collective-permute-start | bytes 442376 | tf_op jit(solution)/shard_map/ppermute | solution.py:232
  505.3 13.5 %collective-permute-start.12 = (bf16[2,2,24,768]{3,2,1,0:T(8,128)(2,1)S(1)}, bf16[2,2,24,768]{3,2,1,0:T(8,128)(2,1)S(1)}, u32[]{:S(2)}, u32[]{:S(2)}) collective-permute-start(bf16[2,2,24,768]{3,2,1,0:T(8,128)(2,1)S(1)} %dynamic-slice_bitcast_fusion.14), channel_id=1, source_target_pairs={{0,8},{1,9},{2,10},{3,11},{4,12},{5,13},{6,14},{7,15},{8,0},{9,1},... | collective-permute-start | bytes 442376 | tf_op jit(solution)/shard_map/ppermute | solution.py:232
  514.3 5.5 collective-permute-start.2
  517.3 5.0 collective-permute-start.23
  518.7 4.5 collective-permute-start.18
  519.8 5.3 collective-permute-start.13
  522.3 4.4 collective-permute-start.3
  523.2 12.1 %collective-permute-start.24 = (bf16[24,768]{1,0:T(8,128)(2,1)S(1)}, bf16[24,768]{1,0:T(8,128)(2,1)S(1)}, u32[]{:S(2)}, u32[]{:S(2)}) collective-permute-start(bf16[24,768]{1,0:T(8,128)(2,1)S(1)} %dynamic-slice_bitcast_fusion.20), channel_id=1, source_target_pairs={{0,4},{1,5},{2,6},{3,7},{4,0},{5,1},{6,2},{7,3},{8,12},{9,13},{10,... | collective-permute-start | bytes 110600 | tf_op jit(solution)/shard_map/ppermute | solution.py:232
  525.1 11.6 %collective-permute-start.19 = (bf16[24,768]{1,0:T(8,128)(2,1)S(1)}, bf16[24,768]{1,0:T(8,128)(2,1)S(1)}, u32[]{:S(2)}, u32[]{:S(2)}) collective-permute-start(bf16[24,768]{1,0:T(8,128)(2,1)S(1)} %dynamic-slice_bitcast_fusion.21), channel_id=1, source_target_pairs={{0,4},{1,5},{2,6},{3,7},{4,0},{5,1},{6,2},{7,3},{8,12},{9,13},{10,... | collective-permute-start | bytes 110600 | tf_op jit(solution)/shard_map/ppermute | solution.py:232
  526.6 10.7 %collective-permute-start.14 = (bf16[24,768]{1,0:T(8,128)(2,1)S(1)}, bf16[24,768]{1,0:T(8,128)(2,1)S(1)}, u32[]{:S(2)}, u32[]{:S(2)}) collective-permute-start(bf16[24,768]{1,0:T(8,128)(2,1)S(1)} %dynamic-slice_bitcast_fusion.22), channel_id=1, source_target_pairs={{0,2},{1,3},{2,0},{3,1},{4,6},{5,7},{6,4},{7,5},{8,10},{9,11},{10,... | collective-permute-start | bytes 110600 | tf_op jit(solution)/shard_map/ppermute | solution.py:232
  530.6 25.5 %collective-permute-start.31 = (bf16[2,2,2,96,768]{4,3,0,1,2:T(8,128)(2,1)S(1)}, bf16[2,2,2,96,768]{4,3,0,1,2:T(8,128)(2,1)S(1)}, u32[]{:S(2)}, u32[]{:S(2)}) collective-permute-start(bf16[2,2,2,96,768]{4,3,0,1,2:T(8,128)(2,1)S(1)} %dynamic-slice_bitcast_fusion), channel_id=1, source_target_pairs={{0,2},{1,3},{2,0},{3,1},{4,6},{5,7},{6,4},{7,5},{8,10},{9,11},{10,... | collective-permute-start | bytes 3538952 | tf_op jit(solution)/shard_map/ppermute | solution.py:232
  534.0 28.3 %collective-permute-start.26 = (bf16[2,2,2,24,3072]{4,3,2,0,1:T(8,128)(2,1)S(1)}, bf16[2,2,2,24,3072]{4,3,2,0,1:T(8,128)(2,1)S(1)}, u32[]{:S(2)}, u32[]{:S(2)}) collective-permute-start(bf16[2,2,2,24,3072]{4,3,2,0,1:T(8,128)(2,1)S(1)} %dynamic-slice_bitcast_fusion.1), channel_id=1, source_target_pairs={{0,4},{1,5},{2,6},{3,7},{4,0},{5,1},{6,2},{7,3},{8,12},{9,13},{10,... | collective-permute-start | bytes 3538952 | tf_op jit(solution)/shard_map/ppermute | solution.py:232
  535.3 28.0 %collective-permute-start.4 = (bf16[24,768]{1,0:T(8,128)(2,1)S(1)}, bf16[24,768]{1,0:T(8,128)(2,1)S(1)}, u32[]{:S(2)}, u32[]{:S(2)}) collective-permute-start(bf16[24,768]{1,0:T(8,128)(2,1)S(1)} %dynamic-slice_bitcast_fusion.23), channel_id=1, source_target_pairs={{0,16},{1,17},{2,18},{3,19},{4,20},{5,21},{6,22},{7,23},{8,24},{9,... | collective-permute-start | bytes 110600 | tf_op jit(solution)/shard_map/ppermute | solution.py:232
  556.4 15.4 %collective-permute-start.32 = (bf16[2,2,96,768]{3,2,0,1:T(8,128)(2,1)S(1)}, bf16[2,2,96,768]{3,2,0,1:T(8,128)(2,1)S(1)}, u32[]{:S(2)}, u32[]{:S(2)}) collective-permute-start(bf16[2,2,96,768]{3,2,0,1:T(8,128)(2,1)S(1)} %dynamic-slice_bitcast_fusion.2), channel_id=1, source_target_pairs={{0,4},{1,5},{2,6},{3,7},{4,0},{5,1},{6,2},{7,3},{8,12},{9,13},{10,... | collective-permute-start | bytes 1769480 | tf_op jit(solution)/shard_map/ppermute | solution.py:232
  562.8 14.3 %collective-permute-start.27 = (bf16[2,2,24,3072]{3,2,1,0:T(8,128)(2,1)S(1)}, bf16[2,2,24,3072]{3,2,1,0:T(8,128)(2,1)S(1)}, u32[]{:S(2)}, u32[]{:S(2)}) collective-permute-start(bf16[2,2,24,3072]{3,2,1,0:T(8,128)(2,1)S(1)} %dynamic-slice_bitcast_fusion.3), channel_id=1, source_target_pairs={{0,8},{1,9},{2,10},{3,11},{4,12},{5,13},{6,14},{7,15},{8,0},{9,1},... | collective-permute-start | bytes 1769480 | tf_op jit(solution)/shard_map/ppermute | solution.py:232
  571.9 10.7 %collective-permute-start.33 = (bf16[2,96,768]{2,1,0:T(8,128)(2,1)S(1)}, bf16[2,96,768]{2,1,0:T(8,128)(2,1)S(1)}, u32[]{:S(2)}, u32[]{:S(2)}) collective-permute-start(bf16[2,96,768]{2,1,0:T(8,128)(2,1)S(1)} %dynamic-slice_bitcast_fusion.4), channel_id=1, source_target_pairs={{0,8},{1,9},{2,10},{3,11},{4,12},{5,13},{6,14},{7,15},{8,0},{9,1},... | collective-permute-start | bytes 884744 | tf_op jit(solution)/shard_map/ppermute | solution.py:232
  577.2 16.3 %collective-permute-start.28 = (bf16[2,24,3072]{2,1,0:T(8,128)(2,1)S(1)}, bf16[2,24,3072]{2,1,0:T(8,128)(2,1)S(1)}, u32[]{:S(2)}, u32[]{:S(2)}) collective-permute-start(bf16[2,24,3072]{2,1,0:T(8,128)(2,1)S(1)} %dynamic-slice_bitcast_fusion.5), channel_id=1, source_target_pairs={{0,16},{1,17},{2,18},{3,19},{4,20},{5,21},{6,22},{7,23},{8,24},{9,... | collective-permute-start | bytes 884744 | tf_op jit(solution)/shard_map/ppermute | solution.py:232
  582.7 12.9 %collective-permute-start.34 = (bf16[96,768]{1,0:T(8,128)(2,1)S(1)}, bf16[96,768]{1,0:T(8,128)(2,1)S(1)}, u32[]{:S(2)}, u32[]{:S(2)}) collective-permute-start(bf16[96,768]{1,0:T(8,128)(2,1)S(1)} %dynamic-slice_bitcast_fusion.10), channel_id=1, source_target_pairs={{0,16},{1,17},{2,18},{3,19},{4,20},{5,21},{6,22},{7,23},{8,24},{9,... | collective-permute-start | bytes 442376 | tf_op jit(solution)/shard_map/ppermute | solution.py:232
  593.6 5.2 collective-permute-start.29
  (28 other events, 146.2 us)
Sparse Core Ops, SparseCore 0:
  15.2 63.8 all-gather.7
  82.0 85.7 all-gather.5
